TPU v7x, 32 devices: a whole 2x2x4 slice. The times are simulated.
32 devices in a mesh: gx: 8 (over y, x, core), gy: 4 (over z).
Axes of the slice: x: 2, y: 2, z: 4, core: 2. Of those that a mesh axis runs over, the one named last changes fastest.
Arguments:
- populations: float32 [19, 64, 64, 128], P(None, 'gx', 'gy'), may hold values from 0.02 to 0.1
- solid: int32 [64, 64, 128], P('gx', 'gy'), may hold values 0 or 1
- visible: int32 [4, 4, 8], replicated, may hold values 0 or 1
- omega: float32 [1], replicated, may hold values from 1 to 1.6
- iso_levels: float32 [8], replicated, may hold values from -1 to 1
- iso_index: int32 [4, 4], replicated, may hold values from 0 to 7
Outputs:
- new_populations: float32 [19, 64, 64, 128], P(None, 'gx', 'gy')
- q_field: float32 [64, 64, 128], P('gx', 'gy')
- crossings: float32 [3, 64, 64, 128], P(None, 'gx', 'gy')
All inputs are finite; a program needn't handle non-finite values. No bound on the sum of `solid` on one device may be relied on, other than what follows from the above.
Results may differ from a plain program's by a relative error of at most 0.000033.
Values sent between devices are 32-bit elements; how exact they have to be, the bound alone decides.
A program may use at most 64 MiB of HBM per device.

v0:
```python
import jax
import jax.numpy as jnp
from jax import lax
from jax.sharding import PartitionSpec as P

BRICK = 16
LEVELS = 8


LATTICE = [
    (0, 0, 0),
    (1, 0, 0),
    (-1, 0, 0),
    (0, 1, 0),
    (0, -1, 0),
    (0, 0, 1),
    (0, 0, -1),
    (1, 1, 0),
    (-1, -1, 0),
    (1, -1, 0),
    (-1, 1, 0),
    (1, 0, 1),
    (-1, 0, -1),
    (1, 0, -1),
    (-1, 0, 1),
    (0, 1, 1),
    (0, -1, -1),
    (0, 1, -1),
    (0, -1, 1),
]
OPPOSITE = [0, 2, 1, 4, 3, 6, 5, 8, 7, 10, 9, 12, 11, 14, 13, 16, 15, 18, 17]
WEIGHTS = [1.0 / 3.0] + [1.0 / 18.0] * 6 + [1.0 / 36.0] * 12


def padded_2(shard, sides, width):
    for axis, dim in sides:
        size, length = (lax.axis_size(axis), shard.shape[dim])
        up = [(i, (i + 1) % size) for i in range(size)]
        down = [(j, i) for i, j in up]
        last = lax.slice_in_dim(shard, length - width, length, axis=dim)
        initial = lax.slice_in_dim(shard, 0, width, axis=dim)
        before = lax.ppermute(last, axis, up)
        after = lax.ppermute(initial, axis, down)
        shard = jnp.concatenate([before, shard, after], axis=dim)
    return shard


def moments(stacked):
    density = stacked[0]
    for number in range(1, 19):
        density = density + stacked[number]
    velocity = []
    for direction in range(3):
        total = jnp.zeros_like(density)
        for number in range(19):
            component = LATTICE[number][direction]
            if component == 1:
                total = total + stacked[number]
            elif component == -1:
                total = total - stacked[number]
        velocity.append(total / density)
    return (density, velocity)


def collide(populations, solid, rate):
    density, velocity = moments(populations)
    speed = velocity[0] * velocity[0] + velocity[1] * velocity[1] + velocity[2] * velocity[2]
    collided = []
    for number in range(19):
        projection = jnp.zeros_like(density)
        for direction in range(3):
            component = LATTICE[number][direction]
            if component == 1:
                projection = projection + velocity[direction]
            elif component == -1:
                projection = projection - velocity[direction]
        equilibrium = (
            WEIGHTS[number]
            * density
            * (1.0 + 3.0 * projection + 4.5 * projection * projection - 1.5 * speed)
        )
        relaxed = populations[number] - rate * (populations[number] - equilibrium)
        collided.append(jnp.where(solid == 1, populations[OPPOSITE[number]], relaxed))
    return collided


def crossing(here, there):
    return jnp.maximum(-here * there, 0.0) / (here * here + there * there + 0.25)


def expand_bricks(table, width_x, width_y):
    start_x = lax.axis_index("gx") * width_x
    start_y = lax.axis_index("gy") * width_y
    rows = lax.dynamic_slice_in_dim(table, start_x // BRICK, max(width_x // BRICK, 1), 0)
    rows = lax.dynamic_slice_in_dim(jnp.repeat(rows, BRICK, axis=0), start_x % BRICK, width_x, 0)
    rows = lax.dynamic_slice_in_dim(rows, start_y // BRICK, max(width_y // BRICK, 1), 1)
    return jnp.repeat(rows, BRICK, axis=1)


def per_device(populations, solid, visible, omega, iso_levels, iso_index):
    width_x = populations.shape[1]
    width_y = populations.shape[2]
    collided = collide(populations, solid, omega[0])
    padded = padded_2(jnp.stack(collided), (("gx", 1), ("gy", 2)), 1)
    read = []
    for number in range(19):
        step_x, step_y, step_z = LATTICE[number]
        plane = padded[number, 1 - step_x : 1 - step_x + width_x, 1 - step_y : 1 - step_y + width_y]
        read.append(jnp.roll(plane, step_z, axis=2))
    new_populations = jnp.stack(read)
    flow_density, flow = moments(read)
    rimmed = padded_2(jnp.stack(flow), (("gx", 1), ("gy", 2)), 3)

    def window(offset_x, offset_y):
        return rimmed[
            :, 3 + offset_x : 4 + offset_x + width_x, 3 + offset_y : 4 + offset_y + width_y, :
        ]

    along_x = (-window(2, 0) + 8.0 * window(1, 0) - 8.0 * window(-1, 0) + window(-2, 0)) / 12.0
    along_y = (-window(0, 2) + 8.0 * window(0, 1) - 8.0 * window(0, -1) + window(0, -2)) / 12.0
    centre = window(0, 0)
    along_z = (
        -jnp.roll(centre, -2, 3)
        + 8.0 * jnp.roll(centre, -1, 3)
        - 8.0 * jnp.roll(centre, 1, 3)
        + jnp.roll(centre, 2, 3)
    ) / 12.0
    grads = [[along_x[first], along_y[first], along_z[first]] for first in range(3)]
    inner = grads[0][0] * grads[0][0] + grads[1][1] * grads[1][1] + grads[2][2] * grads[2][2]
    inner = inner + 2.0 * (
        grads[0][1] * grads[1][0] + grads[0][2] * grads[2][0] + grads[1][2] * grads[2][1]
    )
    scaled = -50.0 * inner
    choose = iso_index[:, :, None] == jnp.arange(LEVELS, dtype=jnp.int32)[None, None, :]
    brick_levels = jnp.sum(jnp.where(choose, iso_levels[None, None, :], 0.0), axis=2)
    level = expand_bricks(brick_levels, width_x, width_y)[:, :, None]
    inside = scaled[:width_x, :width_y]
    here = inside - level
    shown = jnp.repeat(expand_bricks(visible, width_x, width_y), BRICK, axis=2) == 1
    weight_x = crossing(here, scaled[1 : width_x + 1, :width_y] - level)
    weight_y = crossing(here, scaled[:width_x, 1 : width_y + 1] - level)
    weight_z = crossing(here, jnp.roll(inside, -1, 2) - level)
    weights = jnp.stack(
        [
            jnp.where(shown, weight_x, 0.0),
            jnp.where(shown, weight_y, 0.0),
            jnp.where(shown, weight_z, 0.0),
        ]
    )
    q_field = jnp.where(shown, inside, 0.0)
    return (new_populations, q_field, weights)


def solution(mesh):
    in_specs = (P(None, "gx", "gy", None), P("gx", "gy", None), P(), P(), P(), P())
    out_specs = (P(None, "gx", "gy", None), P("gx", "gy", None), P(None, "gx", "gy", None))
    return jax.shard_map(
        per_device, mesh=mesh, in_specs=in_specs, out_specs=out_specs, check_vma=False
    )
```

profile of v0, /device:TPU:0, one launch (start us, length us, event | category | flops | bytes accessed | tf_op | source)
XLA Modules:
  0.0 40.3 jit_solution(16814178140448814718)
XLA Ops:
  1.3 1.5 %constant_dynamic-update-slice_fusion.37 = (f32[19,8,16,128]{3,2,1,0:T(8,128)S(1)}, f32[8,16,128]{2,1,0:T(8,128)S(1)}, f32[8,16,128]{2,1,0:T(8,128)S(1)}, f32[8,...) fusion(f32[]{:T(128)} %bitcast.507, ...), kind=kLoop, calls=%fused_computation.102 | loop fusion | flops 1015807 | bytes 1785860
  2.8 0.1 copy.27
  2.9 1.2 %copy-done = f32[19,8,16,128]{3,2,1,0:T(8,128)S(1)} copy-done((f32[19,8,16,128]{3,2,1,0:T(8,128)S(1)}, f32[19,8,16,128]{3,2,1,0:T(8,128)}, u32[]{:S(2)}) %copy-start) | copy-done | bytes 1245208
  4.7 0.0 copy-start.3
  5.0 3.4 %collective-permute-start.1 = (f32[19,1,16,128]{3,2,1,0:T(8,128)S(1)}, f32[19,1,16,128]{3,2,1,0:T(8,128)S(1)}, u32[]{:S(2)}, u32[]{:S(2)}) collective-permute-start(f32[19,1,16,128]{3,2,1,0:T(8,128)S(1)} %get-tuple-element.48), channel_id=1, source_target_pairs={{4,0},{8,4},{12,8},{16,12},{20,16},{24,20},{28,24},{0,28},{5,1},{9... | collective-permute-start | bytes 466952 | tf_op jit(solution)/shard_map/ppermute | solution.py:43
  8.4 0.2 select_reduce_fusion
  8.5 0.1 slice.511
  8.6 0.1 slice.509
  8.7 0.6 %dynamic_slice.5 = f32[1,1]{1,0:T(1,128)} dynamic-slice(f32[4,4]{1,0:T(4,128)S(1)} %select_reduce_fusion, s32[]{:T(128)S(6)} %select_n.126, s32[]{:T(128)S(6)} %select_n.129), dynamic_slice_sizes={1,1} | dynamic-slice | bytes 12 | tf_op jit(solution)/shard_map/dynamic_slice | solution.py:96
  9.3 0.7 %compare_bitcast_fusion = pred[8]{0:T(512)(128)(4,1)S(1)} fusion(s32[4,4,8]{2,1,0:T(4,128)} %param.8, s32[]{:T(128)S(6)} %select_n.126, s32[]{:T(128)S(6)} %select_n.129), kind=kLoop, calls=%fused_computation.388 | loop fusion | flops 8 | bytes 48 | tf_op jit(solution)/shard_map/eq | solution.py:139
  10.0 0.1 broadcast_in_dim.31
  10.1 0.1 eq.23
  10.1 1.7 %collective-permute-done.1 = f32[19,1,16,128]{3,2,1,0:T(8,128)S(1)} collective-permute-done((f32[19,1,16,128]{3,2,1,0:T(8,128)S(1)}, f32[19,1,16,128]{3,2,1,0:T(8,128)S(1)}, u32[]{:S(2)}, u32[]{:S(2)}) %collective-permute-start.1) | collective-permute-done | bytes 155680 | tf_op jit(solution)/shard_map/ppermute | solution.py:43
  11.9 2.0 %collective-permute-done = f32[19,1,16,128]{3,2,1,0:T(8,128)S(1)} collective-permute-done((f32[19,1,16,128]{3,2,1,0:T(8,128)S(1)}, f32[19,1,16,128]{3,2,1,0:T(8,128)S(1)}, u32[]{:S(2)}, u32[]{:S(2)}) %collective-permute-start) | collective-permute-done | bytes 155680 | tf_op jit(solution)/shard_map/ppermute | solution.py:42
  13.9 0.1 pad_maximum_fusion.4
  14.1 1.6 %collective-permute-start.2 = (f32[19,10,1,128]{3,2,1,0:T(1,128)S(1)}, f32[19,10,1,128]{3,2,1,0:T(1,128)S(1)}, u32[]{:S(2)}, u32[]{:S(2)}) collective-permute-start(f32[19,10,1,128]{3,2,1,0:T(1,128)S(1)} %get-tuple-element.39), channel_id=1, source_target_pairs={{0,1},{1,2},{2,3},{3,0},{4,5},{5,6},{6,7},{7,4},{8,9},{9,10},{10,1... | collective-permute-start | bytes 291848 | tf_op jit(solution)/shard_map/ppermute | solution.py:42
  15.7 2.2 %collective-permute-start.3 = (f32[19,10,1,128]{3,2,1,0:T(1,128)S(1)}, f32[19,10,1,128]{3,2,1,0:T(1,128)S(1)}, u32[]{:S(2)}, u32[]{:S(2)}) collective-permute-start(f32[19,10,1,128]{3,2,1,0:T(1,128)S(1)} %get-tuple-element.40), channel_id=1, source_target_pairs={{1,0},{2,1},{3,2},{0,3},{5,4},{6,5},{7,6},{4,7},{9,8},{10,9},{11,1... | collective-permute-start | bytes 291848 | tf_op jit(solution)/shard_map/ppermute | solution.py:43
  18.0 0.1 slice.519
  18.0 0.1 slice.517
  18.1 0.1 slice.515
  18.2 0.1 slice.513
  18.3 2.3 %collective-permute-done.2 = f32[19,10,1,128]{3,2,1,0:T(1,128)S(1)} collective-permute-done((f32[19,10,1,128]{3,2,1,0:T(1,128)S(1)}, f32[19,10,1,128]{3,2,1,0:T(1,128)S(1)}, u32[]{:S(2)}, u32[]{:S(2)}) %collective-permute-start.2) | collective-permute-done | bytes 97312 | tf_op jit(solution)/shard_map/ppermute | solution.py:42
  20.6 0.7 %collective-permute-done.3 = f32[19,10,1,128]{3,2,1,0:T(1,128)S(1)} collective-permute-done((f32[19,10,1,128]{3,2,1,0:T(1,128)S(1)}, f32[19,10,1,128]{3,2,1,0:T(1,128)S(1)}, u32[]{:S(2)}, u32[]{:S(2)}) %collective-permute-start.3) | collective-permute-done | bytes 97312 | tf_op jit(solution)/shard_map/ppermute | solution.py:43
  21.4 0.1 slice.527
  21.5 0.1 slice.525
  21.5 0.1 slice.523
  21.6 0.1 slice.521
  21.7 0.3 fusion.192
  22.1 0.1 constant_dynamic-update-slice_fusion.32
  22.2 0.1 constant_dynamic-update-slice_fusion.31
  22.4 0.1 fusion.197
  22.6 1.1 %collective-permute-start.5 = (f32[3,3,16,128]{3,2,1,0:T(8,128)S(1)}, f32[3,3,16,128]{3,2,1,0:T(8,128)S(1)}, u32[]{:S(2)}, u32[]{:S(2)}) collective-permute-start(f32[3,3,16,128]{3,2,1,0:T(8,128)S(1)} %get-tuple-element.66), channel_id=1, source_target_pairs={{4,0},{8,4},{12,8},{16,12},{20,16},{24,20},{28,24},{0,28},{5,1},{9... | collective-permute-start | bytes 221192 | tf_op jit(solution)/shard_map/ppermute | solution.py:43
  23.6 2.6 %collective-permute-done.5 = f32[3,3,16,128]{3,2,1,0:T(8,128)S(1)} collective-permute-done((f32[3,3,16,128]{3,2,1,0:T(8,128)S(1)}, f32[3,3,16,128]{3,2,1,0:T(8,128)S(1)}, u32[]{:S(2)}, u32[]{:S(2)}) %collective-permute-start.5) | collective-permute-done | bytes 73760 | tf_op jit(solution)/shard_map/ppermute | solution.py:43
  26.2 2.1 %collective-permute-done.4 = f32[3,3,16,128]{3,2,1,0:T(8,128)S(1)} collective-permute-done((f32[3,3,16,128]{3,2,1,0:T(8,128)S(1)}, f32[3,3,16,128]{3,2,1,0:T(8,128)S(1)}, u32[]{:S(2)}, u32[]{:S(2)}) %collective-permute-start.4) | collective-permute-done | bytes 73760 | tf_op jit(solution)/shard_map/ppermute | solution.py:42
  28.4 2.1 %collective-permute-start.6 = (f32[3,14,3,128]{3,2,1,0:T(4,128)S(1)}, f32[3,14,3,128]{3,2,1,0:T(4,128)S(1)}, u32[]{:S(2)}, u32[]{:S(2)}) collective-permute-start(f32[3,14,3,128]{3,2,1,0:T(4,128)S(1)} %get-tuple-element.61), channel_id=1, source_target_pairs={{1,0},{2,1},{3,2},{0,3},{5,4},{6,5},{7,6},{4,7},{9,8},{10,9},{11,1... | collective-permute-start | bytes 193544 | tf_op jit(solution)/shard_map/ppermute | solution.py:43
  30.5 0.0 copy-start.1
  30.5 3.1 %collective-permute-done.6 = f32[3,14,3,128]{3,2,1,0:T(4,128)S(1)} collective-permute-done((f32[3,14,3,128]{3,2,1,0:T(4,128)S(1)}, f32[3,14,3,128]{3,2,1,0:T(4,128)S(1)}, u32[]{:S(2)}, u32[]{:S(2)}) %collective-permute-start.6) | collective-permute-done | bytes 64544 | tf_op jit(solution)/shard_map/ppermute | solution.py:43
  33.6 3.2 %collective-permute-done.7 = f32[3,14,3,128]{3,2,1,0:T(4,128)S(1)} collective-permute-done((f32[3,14,3,128]{3,2,1,0:T(4,128)S(1)}, f32[3,14,3,128]{3,2,1,0:T(4,128)S(1)}, u32[]{:S(2)}, u32[]{:S(2)}) %collective-permute-start.7) | collective-permute-done | bytes 64544 | tf_op jit(solution)/shard_map/ppermute | solution.py:42
  36.8 0.1 pad_maximum_fusion
  36.8 0.2 fusion.208
  37.0 0.2 fusion.207
  37.2 0.2 fusion.210
  37.3 0.2 fusion.209
  37.5 0.6 %fusion.3 = (f32[3,9,17,128]{3,2,1,0:T(8,128)S(1)}, f32[3,9,17,128]{3,2,1,0:T(8,128)S(1)}, f32[3,9,17,128]{3,2,1,0:T(8,128)S(1)}) fusion(f32[3,14,19,128]{3,2,1,0:T(8,128)S(1)} %get-tuple-element.59, f32[3,14,19,128]{3,2,1,0:T(8,128)S(1)} %get-tuple-element.60, f32[3,9,17,126]{3,2,1,0:T(8,128)S(1)} %get-tuple-element.53, ...), kind=kLoop, calls=%fused_computation.10 | loop fusion | flops 1468800 | bytes 3525120 | tf_op jit(solution)/shard_map/div | solution.py:119
  38.1 0.1 fusion.14
  38.2 0.1 slice.557
  38.3 1.3 %select_bitcast_fusion.2 = (f32[1,8,16,128]{3,2,1,0:T(8,128)S(1)}, f32[1,8,16,128]{3,2,1,0:T(8,128)S(1)}, f32[1,8,16,128]{3,2,1,0:T(8,128)S(1)}, f32[8,16,128]{2,1,0:T(8,128)}) fusion(f32[9,17,128]{2,1,0:T(8,128)S(1)} %fusion.14, f32[]{:T(128)} %bitcast.70, pred[128]{0:T(512)(128)(4,1)S(1)} %eq.23, f32[8,16,1]{2,1,0:T(8,128)S(1)} %slice.558, ...), kind=kLoop, calls=%fused_computation.376 | loop fusion | flops 475136 | bytes 524420 | tf_op jit(solution)/shard_map/stack | solution.py:143
  39.7 0.7 %pad_maximum_fusion.1 = f32[3,8,16,128]{3,2,1,0:T(8,128)} fusion(f32[1,8,16,128]{3,2,1,0:T(8,128)S(1)} %get-tuple-element.68, f32[1,8,16,128]{3,2,1,0:T(8,128)S(1)} %get-tuple-element.69, f32[1,8,16,128]{3,2,1,0:T(8,128)S(1)} %get-tuple-element.67), kind=kLoop, calls=%fused_computation.23 | loop fusion | flops 98304 | bytes 393216 | tf_op jit(solution)/shard_map/stack | solution.py:143
  (48 shorter events, 1.0 us)
Async XLA Ops:
  2.8 1.3 %copy-start = (f32[19,8,16,128]{3,2,1,0:T(8,128)S(1)}, f32[19,8,16,128]{3,2,1,0:T(8,128)}, u32[]{:S(2)}) copy-start(f32[19,8,16,128]{3,2,1,0:T(8,128)} %param.6) | copy-start | bytes 3735556
  4.7 3.6 %copy-start.2 = (s32[4,4]{1,0:T(4,128)S(1)}, s32[4,4]{1,0:T(4,128)}, u32[]{:S(2)}) copy-start(s32[4,4]{1,0:T(4,128)} %param.11) | copy-start | bytes 196
  4.7 3.6 %copy-start.3 = (f32[8]{0:T(128)S(1)}, f32[8]{0:T(128)}, u32[]{:S(2)}) copy-start(f32[8]{0:T(128)} %param.10) | copy-start | bytes 100
  5.0 6.9 %collective-permute-start.1 = (f32[19,1,16,128]{3,2,1,0:T(8,128)S(1)}, f32[19,1,16,128]{3,2,1,0:T(8,128)S(1)}, u32[]{:S(2)}, u32[]{:S(2)}) collective-permute-start(f32[19,1,16,128]{3,2,1,0:T(8,128)S(1)} %get-tuple-element.48), channel_id=1, source_target_pairs={{4,0},{8,4},{12,8},{16,12},{20,16},{24,20},{28,24},{0,28},{5,1},{9... | collective-permute-start | bytes 466952 | tf_op jit(solution)/shard_map/ppermute | solution.py:43
  8.4 5.6 %collective-permute-start = (f32[19,1,16,128]{3,2,1,0:T(8,128)S(1)}, f32[19,1,16,128]{3,2,1,0:T(8,128)S(1)}, u32[]{:S(2)}, u32[]{:S(2)}) collective-permute-start(f32[19,1,16,128]{3,2,1,0:T(8,128)S(1)} %get-tuple-element.47), channel_id=1, source_target_pairs={{0,4},{4,8},{8,12},{12,16},{16,20},{20,24},{24,28},{28,0},{1,5},{5... | collective-permute-start | bytes 466952 | tf_op jit(solution)/shard_map/ppermute | solution.py:42
  14.1 6.6 %collective-permute-start.2 = (f32[19,10,1,128]{3,2,1,0:T(1,128)S(1)}, f32[19,10,1,128]{3,2,1,0:T(1,128)S(1)}, u32[]{:S(2)}, u32[]{:S(2)}) collective-permute-start(f32[19,10,1,128]{3,2,1,0:T(1,128)S(1)} %get-tuple-element.39), channel_id=1, source_target_pairs={{0,1},{1,2},{2,3},{3,0},{4,5},{5,6},{6,7},{7,4},{8,9},{9,10},{10,1... | collective-permute-start | bytes 291848 | tf_op jit(solution)/shard_map/ppermute | solution.py:42
  15.7 5.6 %collective-permute-start.3 = (f32[19,10,1,128]{3,2,1,0:T(1,128)S(1)}, f32[19,10,1,128]{3,2,1,0:T(1,128)S(1)}, u32[]{:S(2)}, u32[]{:S(2)}) collective-permute-start(f32[19,10,1,128]{3,2,1,0:T(1,128)S(1)} %get-tuple-element.40), channel_id=1, source_target_pairs={{1,0},{2,1},{3,2},{0,3},{5,4},{6,5},{7,6},{4,7},{9,8},{10,9},{11,1... | collective-permute-start | bytes 291848 | tf_op jit(solution)/shard_map/ppermute | solution.py:43
  22.6 3.7 %collective-permute-start.5 = (f32[3,3,16,128]{3,2,1,0:T(8,128)S(1)}, f32[3,3,16,128]{3,2,1,0:T(8,128)S(1)}, u32[]{:S(2)}, u32[]{:S(2)}) collective-permute-start(f32[3,3,16,128]{3,2,1,0:T(8,128)S(1)} %get-tuple-element.66), channel_id=1, source_target_pairs={{4,0},{8,4},{12,8},{16,12},{20,16},{24,20},{28,24},{0,28},{5,1},{9... | collective-permute-start | bytes 221192 | tf_op jit(solution)/shard_map/ppermute | solution.py:43
  23.6 4.7 %collective-permute-start.4 = (f32[3,3,16,128]{3,2,1,0:T(8,128)S(1)}, f32[3,3,16,128]{3,2,1,0:T(8,128)S(1)}, u32[]{:S(2)}, u32[]{:S(2)}) collective-permute-start(f32[3,3,16,128]{3,2,1,0:T(8,128)S(1)} %get-tuple-element.65), channel_id=1, source_target_pairs={{0,4},{4,8},{8,12},{12,16},{16,20},{20,24},{24,28},{28,0},{1,5},{5... | collective-permute-start | bytes 221192 | tf_op jit(solution)/shard_map/ppermute | solution.py:42
  28.4 5.2 %collective-permute-start.6 = (f32[3,14,3,128]{3,2,1,0:T(4,128)S(1)}, f32[3,14,3,128]{3,2,1,0:T(4,128)S(1)}, u32[]{:S(2)}, u32[]{:S(2)}) collective-permute-start(f32[3,14,3,128]{3,2,1,0:T(4,128)S(1)} %get-tuple-element.61), channel_id=1, source_target_pairs={{1,0},{2,1},{3,2},{0,3},{5,4},{6,5},{7,6},{4,7},{9,8},{10,9},{11,1... | collective-permute-start | bytes 193544 | tf_op jit(solution)/shard_map/ppermute | solution.py:43
  30.5 6.3 %collective-permute-start.7 = (f32[3,14,3,128]{3,2,1,0:T(4,128)S(1)}, f32[3,14,3,128]{3,2,1,0:T(4,128)S(1)}, u32[]{:S(2)}, u32[]{:S(2)}) collective-permute-start(f32[3,14,3,128]{3,2,1,0:T(4,128)S(1)} %get-tuple-element.62), channel_id=1, source_target_pairs={{0,1},{1,2},{2,3},{3,0},{4,5},{5,6},{6,7},{7,4},{8,9},{9,10},{10,1... | collective-permute-start | bytes 193544 | tf_op jit(solution)/shard_map/ppermute | solution.py:42
  30.5 6.5 %copy-start.1 = (f32[19,8,16,128]{3,2,1,0:T(8,128)}, f32[19,8,16,128]{3,2,1,0:T(8,128)S(1)}, u32[]{:S(2)}) copy-start(f32[19,8,16,128]{3,2,1,0:T(8,128)S(1)} %constant_dynamic-update-slice_fusion.19) | copy-start | bytes 3735556
where the time goes:
time: 40.6 us; the launch traced here: 40.3 us
  waiting for transfers between devices  17.7 us (44%)
  starting transfers between devices  10.4 us (26%)
  other arithmetic  6.75 us (17%)
  local copies, waits for them, and re-layouts  3.75 us (9%)
  between operations  1.66 us (4%)
    ppermute x4, waiting for transfers between devices, padded_2(): before = lax.ppermute(last, axis, up)  9.64 us
    ppermute x4, starting transfers between devices, padded_2(): after = lax.ppermute(initial, axis, down)  8.81 us
    ppermute x4, waiting for transfers between devices, padded_2(): after = lax.ppermute(initial, axis, down)  8.1 us
    unnamed x20, other arithmetic  2.35 us
    another operation x2, other arithmetic, per_device(): jnp.stack([jnp.where(shown, weight_x, 0.0), jnp.where(shown, weight_y, 0....  2.03 us
    ppermute x4, starting transfers between devices, padded_2(): before = lax.ppermute(last, axis, up)  1.64 us
    unnamed x24, local copies, waits for them, and re-layouts  1.4 us
    slice x10, local copies, waits for them, and re-layouts, per_device(): read.append(jnp.roll(plane, step_z, axis=2))  0.82 us
  transfers between devices with their start and end apart: 8, of which 8 were waited for; matrix products, arithmetic and copies ran while one was open for 5% of the time, Pallas kernels for 0%

commit v1 on v0

v1 whole, which is shorter than its diff:
```python
import jax
import jax.numpy as jnp
from jax import lax
from jax.experimental import pallas as pl
from jax.experimental.pallas import tpu as pltpu
from jax.sharding import PartitionSpec as P

BRICK = 16
LATTICE = [
    (0, 0, 0),
    (1, 0, 0),
    (-1, 0, 0),
    (0, 1, 0),
    (0, -1, 0),
    (0, 0, 1),
    (0, 0, -1),
    (1, 1, 0),
    (-1, -1, 0),
    (1, -1, 0),
    (-1, 1, 0),
    (1, 0, 1),
    (-1, 0, -1),
    (1, 0, -1),
    (-1, 0, 1),
    (0, 1, 1),
    (0, -1, -1),
    (0, 1, -1),
    (0, -1, 1),
]
OPPOSITE = [0, 2, 1, 4, 3, 6, 5, 8, 7, 10, 9, 12, 11, 14, 13, 16, 15, 18, 17]
DIRECTIONS = [(-1, 0), (1, 0), (0, -1), (0, 1), (-1, -1), (-1, 1), (1, -1), (1, 1)]
MESH = pl.DeviceIdType.MESH
PAD = 8


def needed_halo(width, height):
    cells = set()
    for x in range(width + 1):
        for y in range(height + 1):
            if x == width and y == height:
                continue
            for step in range(-2, 3):
                cells.add((x + step, y))
                cells.add((x, y + step))
    return {(x, y) for x, y in cells if not (0 <= x < width and 0 <= y < height)}


def message_plan(direction, width, height):
    sx, sy = direction
    halo = needed_halo(width, height)
    pops = [
        k
        for k, c in enumerate(LATTICE)
        if (sx == 0 or c[0] == sx) and (sy == 0 or c[1] == sy)
    ]
    layers, cells = [], []
    if sx and not sy:
        layers = [0, 1, 2] if sx < 0 else [width - 2, width - 1]
    if sy and not sx:
        layers = [0, 1, 2] if sy < 0 else [height - 2, height - 1]
    for x in range(-1, width + 1):
        for y in range(-1, height + 1):
            if (x - sx * width, y - sy * height) not in halo:
                continue
            if sx and sy:
                cells.append((x, y))
            elif sx and 0 <= x < width and not 0 <= y < height:
                cells.append((x, y))
            elif sy and 0 <= y < height and not 0 <= x < width:
                cells.append((x, y))
    return pops, layers, cells


def message_rows(direction, width, height):
    pops, layers, cells = message_plan(direction, width, height)
    line = 1 if direction[0] and direction[1] else (height if direction[0] else width)
    rows = len(pops) * line + 4 * len(layers) * line + 4 * len(cells)
    return -(-rows // 8) * 8


def sums(read):
    n11, n12, n13, n14 = read(11), read(12), read(13), read(14)
    n15, n16, n17, n18 = read(15), read(16), read(17), read(18)
    east = (read(1) + n11) + n13
    west = (read(2) + n12) + n14
    north = (read(3) + n15) + n17
    south = (read(4) + n16) + n18
    n5, n6, n7, n8, n9, n10 = read(5), read(6), read(7), read(8), read(9), read(10)
    density = ((read(0) + n5) + n6) + (east + west) + (north + south) + ((n7 + n8) + (n9 + n10))
    momentum_x = (east - west) + ((n7 - n8) + (n9 - n10))
    momentum_y = (north - south) + ((n7 - n8) - (n9 - n10))
    momentum_z = (n5 - n6) + ((n11 - n12) - (n13 - n14)) + ((n15 - n16) - (n17 - n18))
    return density, momentum_x, momentum_y, momentum_z


def kernel_of(sizes, width, height, depth):
    size_x, size_y = sizes
    plans = [message_plan(d, width, height) for d in DIRECTIONS]

    def kernel(pop_hbm, solid_hbm, visible_hbm, omega_hbm, levels_hbm, index_hbm, new_hbm, q_hbm,
               cross_hbm, pop, solid, visible, omega, levels, index, moved, part, total, flow,
               scaled, q_out, cross_out, *rest):
        sends, recvs = rest[:8], rest[8:16]
        in_sem, send_sem, recv_sem, out_sem = rest[16:]
        ix, iy = lax.axis_index("gx"), lax.axis_index("gy")
        copies = [
            pltpu.make_async_copy(src, dst, in_sem.at[i])
            for i, (src, dst) in enumerate(
                [(pop_hbm, pop), (solid_hbm, solid), (omega_hbm, omega), (visible_hbm, visible),
                 (levels_hbm, levels), (index_hbm, index)]
            )
        ]
        for copy in copies:
            copy.start()
        targets = [
            (lax.rem(ix + sx + size_x, size_x), lax.rem(iy + sy + size_y, size_y))
            for sx, sy in DIRECTIONS
        ]
        barrier = pltpu.get_barrier_semaphore()
        for target in targets:
            pl.semaphore_signal(barrier, inc=1, device_id=target, device_id_type=MESH)

        rows = moved.shape[2]
        blank = jnp.zeros((rows, depth), jnp.float32)

        def clear(x, carry):
            for k in range(19):
                moved[k, x] = blank
            return carry

        lax.fori_loop(0, width + 2, clear, 0)
        for x in (0, width + 3, width + 4):
            for c in range(4):
                total[c, x] = blank
        for copy in copies:
            copy.wait()

        rate = omega[0]
        keep = 1.0 - rate

        def collide(x, carry):
            p = [pop[k, x] for k in range(19)]
            wall = solid[x] == 1
            density, mx, my, mz = sums(lambda k: p[k])
            inverse = 1.0 / density
            velocity = (mx * inverse, my * inverse, mz * inverse)
            base = 1.0 - 1.5 * (
                velocity[0] * velocity[0] + velocity[1] * velocity[1] + velocity[2] * velocity[2]
            )
            scale = rate * density
            heavy, light = scale * (1.0 / 18.0), scale * (1.0 / 36.0)

            def put(k, value):
                cx, cy, cz = LATTICE[k]
                value = jnp.where(wall, p[OPPOSITE[k]], value)
                if cz:
                    value = pltpu.roll(value, cz % depth, 1)
                moved[k, x + (1 + cx), PAD + cy : PAD + cy + height, :] = value

            put(0, keep * p[0] + (scale * (1.0 / 3.0)) * base)
            for k in range(1, 19, 2):
                projection = None
                for direction in range(3):
                    component = LATTICE[k][direction]
                    if component:
                        term = velocity[direction]
                        if projection is None:
                            projection = term if component == 1 else -term
                        else:
                            projection = projection + term if component == 1 else projection - term
                weight = heavy if k < 7 else light
                even = base + 4.5 * (projection * projection)
                odd = 3.0 * projection
                put(k, keep * p[k] + weight * (even + odd))
                put(k + 1, keep * p[k + 1] + weight * (even - odd))
            return carry

        lax.fori_loop(0, width, collide, 0)

        def own_part(x, carry):
            for c, value in enumerate(sums(lambda k: moved[k, x])):
                part[c, x] = value
            return carry

        lax.fori_loop(0, width + 2, own_part, 0)

        def pieces(number):
            sx, sy = DIRECTIONS[number]
            pops, layers, cells = plans[number]
            at, found = 0, []
            from_x = {-1: 0, 0: None, 1: width - 1}[sx]
            from_y = {-1: 0, 0: None, 1: height - 1}[sy]
            for k in pops:
                cx, cy, _ = LATTICE[k]
                if sy == 0:
                    y = slice(PAD + cy, PAD + cy + height)
                    here, there = (k, from_x + cx + 1, y), (k, from_x + cx + 1 - sx * width, y)
                    length = height
                elif sx == 0:
                    x = slice(1 + cx, 1 + cx + width)
                    here = (k, x, PAD + from_y + cy)
                    there = (k, x, PAD + from_y + cy - sy * height)
                    length = width
                else:
                    x, y = from_x + cx + 1, PAD + from_y + cy
                    here = (k, x, slice(y, y + 1))
                    there = (k, x - sx * width, slice(y - sy * height, y - sy * height + 1))
                    length = 1
                found.append((True, at, length, here, there))
                at += length
            for layer in layers:
                for c in range(4):
                    if sy == 0:
                        y = slice(PAD, PAD + height)
                        here, there = (c, layer + 1, y), (c, layer + 2 - sx * width, y)
                        length = height
                    else:
                        here = (c, slice(1, 1 + width), PAD + layer)
                        there = (c, slice(2, 2 + width), PAD + layer - sy * height)
                        length = width
                    found.append((False, at, length, here, there))
                    at += length
            for x, y in cells:
                for c in range(4):
                    here = (c, x + 1, slice(PAD + y, PAD + y + 1))
                    to = PAD + y - sy * height
                    found.append((False, at, 1, here, (c, x + 2 - sx * width, slice(to, to + 1))))
                    at += 1
            return found

        pl.semaphore_wait(barrier, 8)
        remote = []
        for number in (4, 5, 6, 7, 2, 3, 0, 1):
            for is_pop, at, length, here, _ in pieces(number):
                source = moved if is_pop else part
                sends[number][at : at + length, :] = source[here]
            copy = pltpu.make_async_remote_copy(
                src_ref=sends[number],
                dst_ref=recvs[number],
                send_sem=send_sem.at[number],
                recv_sem=recv_sem.at[number],
                device_id=targets[number],
                device_id_type=MESH,
            )
            copy.start()
            remote.append((number, copy))

        for number, copy in remote:
            copy.wait_recv()
            for is_pop, at, length, _, there in pieces(number):
                if is_pop:
                    moved[there] = recvs[number][at : at + length, :]

        new_copy = pltpu.make_async_copy(
            moved.at[:, 1 : 1 + width, PAD : PAD + height, :], new_hbm, out_sem.at[0]
        )
        new_copy.start()

        def all_part(x, carry):
            for c, value in enumerate(sums(lambda k: moved[k, x])):
                total[c, x + 1] = value
            return carry

        lax.fori_loop(0, width + 2, all_part, 0)
        for number in range(8):
            for is_pop, at, length, _, there in pieces(number):
                if not is_pop:
                    total[there] = total[there] + recvs[number][at : at + length, :]

        def divide(x, carry):
            inverse = 1.0 / total[0, x]
            for a in range(3):
                flow[a, x, 0:rows, :] = total[a + 1, x] * inverse
            return carry

        lax.fori_loop(0, width + 5, divide, 0)

        tall = height + 8

        def criterion(x, carry):
            grads = []
            for a in range(3):
                def at(dx, dy):
                    return flow[a, x + 2 + dx, PAD + dy : PAD + dy + tall, :]

                centre = at(0, 0)
                along_x = 8.0 * (at(1, 0) - at(-1, 0)) - (at(2, 0) - at(-2, 0))
                along_y = 8.0 * (at(0, 1) - at(0, -1)) - (at(0, 2) - at(0, -2))
                along_z = 8.0 * (
                    pltpu.roll(centre, depth - 1, 1) - pltpu.roll(centre, 1, 1)
                ) - (pltpu.roll(centre, depth - 2, 1) - pltpu.roll(centre, 2, 1))
                grads.append((along_x, along_y, along_z))
            inner = grads[0][0] * grads[0][0] + grads[1][1] * grads[1][1] + grads[2][2] * grads[2][2]
            inner = inner + 2.0 * (
                grads[0][1] * grads[1][0] + grads[0][2] * grads[2][0] + grads[1][2] * grads[2][1]
            )
            scaled[x] = (-50.0 / 144.0) * inner
            return carry

        lax.fori_loop(0, width + 1, criterion, 0)

        brick_x, brick_y = (ix * width) // BRICK, (iy * height) // BRICK
        chosen = index[brick_x, brick_y]
        level = jnp.float32(0.0)
        for number in range(levels.shape[0]):
            level = jnp.where(chosen == number, levels[number], level)
        lane = lax.broadcasted_iota(jnp.int32, (height, depth), 1) // BRICK
        seen = jnp.zeros((height, depth), jnp.int32)
        for number in range(depth // BRICK):
            seen = jnp.where(lane == number, visible[brick_x, brick_y, number], seen)
        shown = seen == 1

        def edges(x, carry):
            inside = scaled[x, 0:height, :]
            here = inside - level
            square = here * here + 0.25
            q_out[x] = jnp.where(shown, inside, 0.0)
            theres = (
                scaled[x + 1, 0:height, :] - level,
                scaled[x, 1 : 1 + height, :] - level,
                pltpu.roll(here, depth - 1, 1),
            )
            for direction, there in enumerate(theres):
                weight = jnp.maximum(-here * there, 0.0) / (square + there * there)
                cross_out[direction, x] = jnp.where(shown, weight, 0.0)
            return carry

        lax.fori_loop(0, width, edges, 0)
        last = [
            pltpu.make_async_copy(q_out, q_hbm, out_sem.at[1]),
            pltpu.make_async_copy(cross_out, cross_hbm, out_sem.at[2]),
        ]
        for copy in last:
            copy.start()
        for _, copy in remote:
            copy.wait_send()
        new_copy.wait()
        for copy in last:
            copy.wait()

    return kernel


def solution(mesh):
    sizes = (mesh.shape["gx"], mesh.shape["gy"])

    def per_device(populations, solid, visible, omega, iso_levels, iso_index):
        _, width, height, depth = populations.shape
        rows = PAD + height + 8
        f32 = jnp.float32
        messages = [
            pltpu.VMEM((message_rows(d, width, height), depth), f32) for d in DIRECTIONS
        ]
        anywhere = pl.BlockSpec(memory_space=pl.ANY)
        return pl.pallas_call(
            kernel_of(sizes, width, height, depth),
            out_shape=(
                jax.ShapeDtypeStruct(populations.shape, f32),
                jax.ShapeDtypeStruct((width, height, depth), f32),
                jax.ShapeDtypeStruct((3, width, height, depth), f32),
            ),
            in_specs=[anywhere] * 6,
            out_specs=(anywhere,) * 3,
            scratch_shapes=[
                pltpu.VMEM(populations.shape, f32),
                pltpu.VMEM(solid.shape, jnp.int32),
                pltpu.SMEM(visible.shape, jnp.int32),
                pltpu.SMEM(omega.shape, f32),
                pltpu.SMEM(iso_levels.shape, f32),
                pltpu.SMEM(iso_index.shape, jnp.int32),
                pltpu.VMEM((19, width + 2, rows, depth), f32),
                pltpu.VMEM((4, width + 2, rows, depth), f32),
                pltpu.VMEM((4, width + 5, rows, depth), f32),
                pltpu.VMEM((3, width + 5, rows + 8, depth), f32),
                pltpu.VMEM((width + 1, height + 8, depth), f32),
                pltpu.VMEM((width, height, depth), f32),
                pltpu.VMEM((3, width, height, depth), f32),
            ]
            + messages
            + messages
            + [
                pltpu.SemaphoreType.DMA((6,)),
                pltpu.SemaphoreType.DMA((8,)),
                pltpu.SemaphoreType.DMA((8,)),
                pltpu.SemaphoreType.DMA((3,)),
            ],
            compiler_params=pltpu.CompilerParams(
                collective_id=0, has_side_effects=True, vmem_limit_bytes=40 * 1024 * 1024
            ),
        )(populations, solid, visible, omega, iso_levels, iso_index)

    in_specs = (P(None, "gx", "gy", None), P("gx", "gy", None), P(), P(), P(), P())
    out_specs = (P(None, "gx", "gy", None), P("gx", "gy", None), P(None, "gx", "gy", None))
    return jax.shard_map(
        per_device, mesh=mesh, in_specs=in_specs, out_specs=out_specs, check_vma=False
    )
```

time: 40.6 us -> 23.7 us (0.58)
  waiting for transfers between devices: 17.7 us -> 0 us
  Pallas kernels: 0 us -> 15.6 us
  starting transfers between devices: 10.4 us -> 0 us
  other arithmetic: 6.75 us -> 0 us
  local copies, waits for them, and re-layouts: 3.75 us -> 6.5 us
    ppermute x8 -> x0, waiting for transfers between devices: 17.7 us -> none  [the longest x4 9.64 us: padded_2(): before = lax.ppermute(last, axis, up)]
    pallas_call x0 -> x1, Pallas kernels: none -> 15.6 us  [per_device(): pl.pallas_call(kernel_of(sizes, width, height, depth), out_shape=(jax.Sha...]
    ppermute x8 -> x0, starting transfers between devices: 10.4 us -> none  [the longest x4 8.81 us: padded_2(): after = lax.ppermute(initial, axis, down)]
    unnamed x24 -> x13, local copies, waits for them, and re-layouts: 1.4 us -> 6.5 us
    another operation x5 -> x0, other arithmetic: 2.53 us -> none  [the longest x2 2.03 us: per_device(): jnp.stack([jnp.where(shown, weight_x, 0.0), jnp.where(shown, weight_y, 0....]
    unnamed x20 -> x0, other arithmetic: 2.35 us -> none
    slice x17 -> x0, local copies, waits for them, and re-layouts: 1.58 us -> none  [the longest x10 0.82 us: per_device(): read.append(jnp.roll(plane, step_z, axis=2))]
    eq x1 -> x0, other arithmetic: 0.69 us -> none  [per_device(): jnp.repeat(expand_bricks(visible, width_x, width_y), BRICK, axis=2) == 1]
  transfers between devices with their start and end apart: 8 -> 0, of which waited for: 8 -> 0; matrix products, arithmetic and copies ran while one was open for 5% -> 0% of each run, Pallas kernels for 0% -> 0%
where the time goes in v1:
time: 23.7 us; the launch traced here: 23.4 us
  Pallas kernels  15.6 us (66%)
  local copies, waits for them, and re-layouts  6.5 us (27%)
  between operations  1.3 us (5%)
    pallas_call x1, Pallas kernels, per_device(): pl.pallas_call(kernel_of(sizes, width, height, depth), out_shape=(jax.Sha...  15.6 us
    unnamed x13, local copies, waits for them, and re-layouts  6.5 us

profile of v1, /device:TPU:0, one launch (start us, length us, event | category | flops | bytes accessed | tf_op | source)
XLA Modules:
  0.0 23.4 jit_solution(17240404537864925658)
XLA Ops:
  1.3 0.0 copy-start
  1.3 1.3 %copy-done = f32[19,8,16,128]{3,2,1,0:T(8,128)S(1)} copy-done((f32[19,8,16,128]{3,2,1,0:T(8,128)S(1)}, f32[19,8,16,128]{3,2,1,0:T(8,128)}, u32[]{:S(2)}) %copy-start) | copy-done | bytes 1245208
  2.6 0.0 copy-start.1
  2.6 0.8 %copy-done.1 = s32[8,16,128]{2,1,0:T(8,128)S(1)} copy-done((s32[8,16,128]{2,1,0:T(8,128)S(1)}, s32[8,16,128]{2,1,0:T(8,128)}, u32[]{:S(2)}) %copy-start.1) | copy-done | bytes 65560
  3.4 0.0 copy-start.2
  3.4 0.7 %copy-done.2 = s32[4,4,8]{2,1,0:T(4,128)S(1)} copy-done((s32[4,4,8]{2,1,0:T(4,128)S(1)}, s32[4,4,8]{2,1,0:T(4,128)}, u32[]{:S(2)}) %copy-start.2) | copy-done | bytes 536
  4.1 0.0 copy-start.3
  4.1 0.7 %copy-done.3 = s32[4,4]{1,0:T(4,128)S(1)} copy-done((s32[4,4]{1,0:T(4,128)S(1)}, s32[4,4]{1,0:T(4,128)}, u32[]{:S(2)}) %copy-start.3) | copy-done | bytes 88
  4.8 0.0 copy-start.4
  4.8 0.7 %copy-done.4 = f32[8]{0:T(128)S(1)} copy-done((f32[8]{0:T(128)S(1)}, f32[8]{0:T(128)}, u32[]{:S(2)}) %copy-start.4) | copy-done | bytes 56
  5.4 15.6 %shard_map.85 = (f32[19,8,16,128]{3,2,1,0:T(8,128)S(1)}, f32[8,16,128]{2,1,0:T(8,128)S(1)}, f32[3,8,16,128]{3,2,1,0:T(8,128)S(1)}) custom-call(f32[19,8,16,128]{3,2,1,0:T(8,128)S(1)} %copy-done, s32[8,16,128]{2,1,0:T(8,128)S(1)} %copy-done.1, s32[4,4,8]{2,1,0:T(4,128)S(1)} %copy-done.2, f32[1]{0:T(128)S(6)} %copy.12.omega_hbm, f32[8]{0:T(128)S(1)} %copy-done.4, ...), custom_call_target="tpu_custom_call" | custom-call | tf_op jit(solution)/shard_map/pallas_call | solution.py:355
  21.1 1.0 %copy.13 = f32[19,8,16,128]{3,2,1,0:T(8,128)} copy(f32[19,8,16,128]{3,2,1,0:T(8,128)S(1)} %get-tuple-element.6) | data formatting | bytes 2490368
  22.1 0.6 %copy.14 = f32[8,16,128]{2,1,0:T(8,128)} copy(f32[8,16,128]{2,1,0:T(8,128)S(1)} %get-tuple-element.7) | data formatting | bytes 131072
  22.8 0.7 %copy.15 = f32[3,8,16,128]{3,2,1,0:T(8,128)} copy(f32[3,8,16,128]{3,2,1,0:T(8,128)S(1)} %get-tuple-element.8) | data formatting | bytes 393216
Async XLA Ops:
  1.3 1.3 %copy-start = (f32[19,8,16,128]{3,2,1,0:T(8,128)S(1)}, f32[19,8,16,128]{3,2,1,0:T(8,128)}, u32[]{:S(2)}) copy-start(f32[19,8,16,128]{3,2,1,0:T(8,128)} %pop_hbm.1) | copy-start | bytes 3735556
  2.6 0.8 %copy-start.1 = (s32[8,16,128]{2,1,0:T(8,128)S(1)}, s32[8,16,128]{2,1,0:T(8,128)}, u32[]{:S(2)}) copy-start(s32[8,16,128]{2,1,0:T(8,128)} %solid_hbm.1) | copy-start | bytes 196612
  3.4 0.7 %copy-start.2 = (s32[4,4,8]{2,1,0:T(4,128)S(1)}, s32[4,4,8]{2,1,0:T(4,128)}, u32[]{:S(2)}) copy-start(s32[4,4,8]{2,1,0:T(4,128)} %visible_hbm.1) | copy-start | bytes 1540
  4.1 0.7 %copy-start.3 = (s32[4,4]{1,0:T(4,128)S(1)}, s32[4,4]{1,0:T(4,128)}, u32[]{:S(2)}) copy-start(s32[4,4]{1,0:T(4,128)} %index_hbm.1) | copy-start | bytes 196
  4.8 0.7 %copy-start.4 = (f32[8]{0:T(128)S(1)}, f32[8]{0:T(128)}, u32[]{:S(2)}) copy-start(f32[8]{0:T(128)} %levels_hbm.1) | copy-start | bytes 100

commit v2 on v1

--- a/solution.py
+++ b/solution.py
@@ -97,17 +97,14 @@
     size_x, size_y = sizes
     plans = [message_plan(d, width, height) for d in DIRECTIONS]
 
-    def kernel(pop_hbm, solid_hbm, visible_hbm, omega_hbm, levels_hbm, index_hbm, new_hbm, q_hbm,
-               cross_hbm, pop, solid, visible, omega, levels, index, moved, part, total, flow,
-               scaled, q_out, cross_out, *rest):
+    def kernel(pop_hbm, solid_hbm, omega_hbm, moved, total, pop, solid, omega, *rest):
         sends, recvs = rest[:8], rest[8:16]
-        in_sem, send_sem, recv_sem, out_sem = rest[16:]
+        in_sem, send_sem, recv_sem = rest[16:]
         ix, iy = lax.axis_index("gx"), lax.axis_index("gy")
         copies = [
             pltpu.make_async_copy(src, dst, in_sem.at[i])
             for i, (src, dst) in enumerate(
-                [(pop_hbm, pop), (solid_hbm, solid), (omega_hbm, omega), (visible_hbm, visible),
-                 (levels_hbm, levels), (index_hbm, index)]
+                [(pop_hbm, pop), (solid_hbm, solid), (omega_hbm, omega)]
             )
         ]
         for copy in copies:
@@ -179,7 +176,7 @@
 
         def own_part(x, carry):
             for c, value in enumerate(sums(lambda k: moved[k, x])):
-                part[c, x] = value
+                total[c, x + 1] = value
             return carry
 
         lax.fori_loop(0, width + 2, own_part, 0)
@@ -212,17 +209,17 @@
                 for c in range(4):
                     if sy == 0:
                         y = slice(PAD, PAD + height)
-                        here, there = (c, layer + 1, y), (c, layer + 2 - sx * width, y)
+                        here, there = (c, layer + 2, y), (c, layer + 2 - sx * width, y)
                         length = height
                     else:
-                        here = (c, slice(1, 1 + width), PAD + layer)
+                        here = (c, slice(2, 2 + width), PAD + layer)
                         there = (c, slice(2, 2 + width), PAD + layer - sy * height)
                         length = width
                     found.append((False, at, length, here, there))
                     at += length
             for x, y in cells:
                 for c in range(4):
-                    here = (c, x + 1, slice(PAD + y, PAD + y + 1))
+                    here = (c, x + 2, slice(PAD + y, PAD + y + 1))
                     to = PAD + y - sy * height
                     found.append((False, at, 1, here, (c, x + 2 - sx * width, slice(to, to + 1))))
                     at += 1
@@ -232,7 +229,7 @@
         remote = []
         for number in (4, 5, 6, 7, 2, 3, 0, 1):
             for is_pop, at, length, here, _ in pieces(number):
-                source = moved if is_pop else part
+                source = moved if is_pop else total
                 sends[number][at : at + length, :] = source[here]
             copy = pltpu.make_async_remote_copy(
                 src_ref=sends[number],
@@ -245,27 +242,58 @@
             copy.start()
             remote.append((number, copy))
 
-        for number, copy in remote:
-            copy.wait_recv()
+        remote = dict(remote)
+        for number in (0, 1, 4, 5, 6, 7, 2, 3):
+            remote[number].wait_recv()
+            groups = {}
             for is_pop, at, length, _, there in pieces(number):
-                if is_pop:
-                    moved[there] = recvs[number][at : at + length, :]
-
+                value = recvs[number][at : at + length, :]
+                if not is_pop:
+                    total[there] = total[there] + value
+                    continue
+                moved[there] = value
+                k, x, y = there
+                x = slice(x.start + 1, x.stop + 1) if isinstance(x, slice) else x + 1
+                groups.setdefault(LATTICE[k][:2], []).append((LATTICE[k][2], value, x, y))
+            for (cx, cy), members in groups.items():
+                _, value, x, y = members[0]
+                along_z = None
+                for cz, other, _, _ in members[1:]:
+                    value = value + other
+                if len(members) == 3:
+                    up = [other for cz, other, _, _ in members if cz == 1][0]
+                    down = [other for cz, other, _, _ in members if cz == -1][0]
+                    along_z = up - down
+                total[0, x, y] = total[0, x, y] + value
+                for c, sign in ((1, cx), (2, cy)):
+                    if sign:
+                        total[c, x, y] = total[c, x, y] + (value if sign == 1 else -value)
+                if along_z is not None:
+                    total[3, x, y] = total[3, x, y] + along_z
+
+        for copy in remote.values():
+            copy.wait_send()
+
+    return kernel
+
+
+def finish_of(width, height, depth):
+    def kernel(moved, total, visible_hbm, levels_hbm, index_hbm, new_hbm, q_hbm, cross_hbm,
+               visible, levels, index, flow, scaled, q_out, cross_out, in_sem, out_sem):
         new_copy = pltpu.make_async_copy(
             moved.at[:, 1 : 1 + width, PAD : PAD + height, :], new_hbm, out_sem.at[0]
         )
         new_copy.start()
-
-        def all_part(x, carry):
-            for c, value in enumerate(sums(lambda k: moved[k, x])):
-                total[c, x + 1] = value
-            return carry
-
-        lax.fori_loop(0, width + 2, all_part, 0)
-        for number in range(8):
-            for is_pop, at, length, _, there in pieces(number):
-                if not is_pop:
-                    total[there] = total[there] + recvs[number][at : at + length, :]
+        copies = [
+            pltpu.make_async_copy(src, dst, in_sem.at[i])
+            for i, (src, dst) in enumerate(
+                [(visible_hbm, visible), (levels_hbm, levels), (index_hbm, index)]
+            )
+        ]
+        for copy in copies:
+            copy.start()
+        ix, iy = lax.axis_index("gx"), lax.axis_index("gy")
+        rows = total.shape[2]
 
         def divide(x, carry):
             inverse = 1.0 / total[0, x]
@@ -299,6 +327,8 @@
 
         lax.fori_loop(0, width + 1, criterion, 0)
 
+        for copy in copies:
+            copy.wait()
         brick_x, brick_y = (ix * width) // BRICK, (iy * height) // BRICK
         chosen = index[brick_x, brick_y]
         level = jnp.float32(0.0)
@@ -332,8 +362,6 @@
         ]
         for copy in last:
             copy.start()
-        for _, copy in remote:
-            copy.wait_send()
         new_copy.wait()
         for copy in last:
             copy.wait()
@@ -351,43 +379,58 @@
         messages = [
             pltpu.VMEM((message_rows(d, width, height), depth), f32) for d in DIRECTIONS
         ]
-        anywhere = pl.BlockSpec(memory_space=pl.ANY)
+        far = pl.BlockSpec(memory_space=pltpu.HBM)
+        near = pl.BlockSpec(memory_space=pltpu.VMEM)
+        moved, total = pl.pallas_call(
+            kernel_of(sizes, width, height, depth),
+            out_shape=(
+                jax.ShapeDtypeStruct((19, width + 2, rows, depth), f32),
+                jax.ShapeDtypeStruct((4, width + 5, rows, depth), f32),
+            ),
+            in_specs=[far] * 3,
+            out_specs=(near, near),
+            scratch_shapes=[
+                pltpu.VMEM(populations.shape, f32),
+                pltpu.VMEM(solid.shape, jnp.int32),
+                pltpu.SMEM(omega.shape, f32),
+            ]
+            + messages
+            + messages
+            + [
+                pltpu.SemaphoreType.DMA((3,)),
+                pltpu.SemaphoreType.DMA((8,)),
+                pltpu.SemaphoreType.DMA((8,)),
+            ],
+            compiler_params=pltpu.CompilerParams(
+                collective_id=0, has_side_effects=True, vmem_limit_bytes=24 * 1024 * 1024
+            ),
+        )(
+            pltpu.with_memory_space_constraint(populations, pltpu.HBM),
+            pltpu.with_memory_space_constraint(solid, pltpu.HBM),
+            omega,
+        )
         return pl.pallas_call(
-            kernel_of(sizes, width, height, depth),
+            finish_of(width, height, depth),
             out_shape=(
                 jax.ShapeDtypeStruct(populations.shape, f32),
                 jax.ShapeDtypeStruct((width, height, depth), f32),
                 jax.ShapeDtypeStruct((3, width, height, depth), f32),
             ),
-            in_specs=[anywhere] * 6,
-            out_specs=(anywhere,) * 3,
+            in_specs=[near, near, far, far, far],
+            out_specs=(far, far, far),
             scratch_shapes=[
-                pltpu.VMEM(populations.shape, f32),
-                pltpu.VMEM(solid.shape, jnp.int32),
                 pltpu.SMEM(visible.shape, jnp.int32),
-                pltpu.SMEM(omega.shape, f32),
                 pltpu.SMEM(iso_levels.shape, f32),
                 pltpu.SMEM(iso_index.shape, jnp.int32),
-                pltpu.VMEM((19, width + 2, rows, depth), f32),
-                pltpu.VMEM((4, width + 2, rows, depth), f32),
-                pltpu.VMEM((4, width + 5, rows, depth), f32),
                 pltpu.VMEM((3, width + 5, rows + 8, depth), f32),
                 pltpu.VMEM((width + 1, height + 8, depth), f32),
                 pltpu.VMEM((width, height, depth), f32),
                 pltpu.VMEM((3, width, height, depth), f32),
-            ]
-            + messages
-            + messages
-            + [
-                pltpu.SemaphoreType.DMA((6,)),
-                pltpu.SemaphoreType.DMA((8,)),
-                pltpu.SemaphoreType.DMA((8,)),
+                pltpu.SemaphoreType.DMA((3,)),
                 pltpu.SemaphoreType.DMA((3,)),
             ],
-            compiler_params=pltpu.CompilerParams(
-                collective_id=0, has_side_effects=True, vmem_limit_bytes=40 * 1024 * 1024
-            ),
-        )(populations, solid, visible, omega, iso_levels, iso_index)
+            compiler_params=pltpu.CompilerParams(vmem_limit_bytes=24 * 1024 * 1024),
+        )(moved, total, visible, iso_levels, iso_index)
 
     in_specs = (P(None, "gx", "gy", None), P("gx", "gy", None), P(), P(), P(), P())
     out_specs = (P(None, "gx", "gy", None), P("gx", "gy", None), P(None, "gx", "gy", None))

time: 23.7 us -> 17.2 us (0.73)
  local copies, waits for them, and re-layouts: 6.5 us -> 0.01 us
    unnamed x13 -> x6, local copies, waits for them, and re-layouts: 6.5 us -> 0.01 us
    pallas_call x0 -> x1, Pallas kernels: none -> 2.58 us  [per_device(): pl.pallas_call(finish_of(width, height, depth), out_shape=(jax.ShapeDtype...]
    pallas_call x1, Pallas kernels: 15.6 us -> 13 us  [per_device(): pl.pallas_call(kernel_of(sizes, width, height, depth), out_shape=(jax.Sha...]
where the time goes in v2:
time: 17.2 us; the launch traced here: 17 us
  Pallas kernels  15.6 us (91%)
  between operations  1.36 us (8%)
    pallas_call x1, Pallas kernels, per_device(): pl.pallas_call(kernel_of(sizes, width, height, depth), out_shape=(jax.Sha...  13 us
    pallas_call x1, Pallas kernels, per_device(): pl.pallas_call(finish_of(width, height, depth), out_shape=(jax.ShapeDtype...  2.58 us

profile of v2, /device:TPU:0, one launch (start us, length us, event | category | flops | bytes accessed | tf_op | source)
XLA Modules:
  0.0 17.0 jit_solution(12232218452273935600)
XLA Ops:
  0.6 0.0 copy-start.1
  0.6 0.0 copy-start.2
  0.7 0.0 copy-start
  1.3 13.0 %shard_map.85 = (f32[19,10,32,128]{3,2,1,0:T(8,128)S(1)}, f32[4,13,32,128]{3,2,1,0:T(8,128)S(1)}) custom-call(f32[19,8,16,128]{3,2,1,0:T(8,128)} %pop_hbm.1, s32[8,16,128]{2,1,0:T(8,128)} %solid_hbm.1, f32[1]{0:T(128)S(6)} %copy.9.omega_hbm), custom_call_target="tpu_custom_call" | custom-call | tf_op jit(solution)/shard_map/pallas_call | solution.py:384
  14.4 0.0 copy-done.1
  14.4 0.0 copy-done.2
  14.4 0.0 copy-done
  14.4 2.6 %shard_map.86 = (f32[19,8,16,128]{3,2,1,0:T(8,128)}, f32[8,16,128]{2,1,0:T(8,128)}, f32[3,8,16,128]{3,2,1,0:T(8,128)}) custom-call(f32[19,10,32,128]{3,2,1,0:T(8,128)S(1)} %get-tuple-element.5.moved, f32[4,13,32,128]{3,2,1,0:T(8,128)S(1)} %get-tuple-element.6.total, s32[4,4,8]{2,1,0:T(4,128)S(1)} %copy-done, f32[8]{0:T(128)S(1)} %copy-done.2, ...), custom_call_target="tpu_custom_call" | custom-call | tf_op jit(solution)/shard_map/pallas_call | solution.py:412
Async XLA Ops:
  0.6 13.8 %copy-start.1 = (s32[4,4]{1,0:T(4,128)S(1)}, s32[4,4]{1,0:T(4,128)}, u32[]{:S(2)}) copy-start(s32[4,4]{1,0:T(4,128)} %index_hbm.1) | copy-start | bytes 196
  0.6 13.8 %copy-start.2 = (f32[8]{0:T(128)S(1)}, f32[8]{0:T(128)}, u32[]{:S(2)}) copy-start(f32[8]{0:T(128)} %levels_hbm.1) | copy-start | bytes 100
  0.7 13.8 %copy-start = (s32[4,4,8]{2,1,0:T(4,128)S(1)}, s32[4,4,8]{2,1,0:T(4,128)}, u32[]{:S(2)}) copy-start(s32[4,4,8]{2,1,0:T(4,128)} %visible_hbm.1) | copy-start | bytes 1540

commit v3 on v2

--- a/solution.py
+++ b/solution.py
@@ -30,6 +30,7 @@
 OPPOSITE = [0, 2, 1, 4, 3, 6, 5, 8, 7, 10, 9, 12, 11, 14, 13, 16, 15, 18, 17]
 DIRECTIONS = [(-1, 0), (1, 0), (0, -1), (0, 1), (-1, -1), (-1, 1), (1, -1), (1, 1)]
 MESH = pl.DeviceIdType.MESH
+CHUNKS = 4
 PAD = 8
 
 
@@ -71,8 +72,19 @@
     return pops, layers, cells
 
 
-def message_rows(direction, width, height):
+UNITS = (
+    [(number, True, False) for number in (2, 3, 0, 1)]
+    + [(number, True, True) for number in (4, 5, 6, 7)]
+    + [(number, False, True) for number in (2, 3, 0, 1)]
+)
+
+
+def message_rows(unit, width, height):
+    number, with_pops, with_sums = unit
+    direction = DIRECTIONS[number]
     pops, layers, cells = message_plan(direction, width, height)
+    pops = pops if with_pops else []
+    layers, cells = (layers, cells) if with_sums else ([], [])
     line = 1 if direction[0] and direction[1] else (height if direction[0] else width)
     rows = len(pops) * line + 4 * len(layers) * line + 4 * len(cells)
     return -(-rows // 8) * 8
@@ -98,13 +110,19 @@
     plans = [message_plan(d, width, height) for d in DIRECTIONS]
 
     def kernel(pop_hbm, solid_hbm, omega_hbm, moved, total, pop, solid, omega, *rest):
-        sends, recvs = rest[:8], rest[8:16]
-        in_sem, send_sem, recv_sem = rest[16:]
+        count = len(UNITS)
+        sends, recvs = rest[:count], rest[count : 2 * count]
+        in_sem, send_sem, recv_sem = rest[2 * count :]
         ix, iy = lax.axis_index("gx"), lax.axis_index("gy")
+        layers = width // CHUNKS
         copies = [
             pltpu.make_async_copy(src, dst, in_sem.at[i])
             for i, (src, dst) in enumerate(
-                [(pop_hbm, pop), (solid_hbm, solid), (omega_hbm, omega)]
+                [(solid_hbm, solid), (omega_hbm, omega)]
+                + [
+                    (pop_hbm.at[:, pl.ds(c * layers, layers)], pop.at[:, pl.ds(c * layers, layers)])
+                    for c in range(CHUNKS)
+                ]
             )
         ]
         for copy in copies:
@@ -129,7 +147,7 @@
         for x in (0, width + 3, width + 4):
             for c in range(4):
                 total[c, x] = blank
-        for copy in copies:
+        for copy in copies[:2]:
             copy.wait()
 
         rate = omega[0]
@@ -172,18 +190,17 @@
                 put(k + 1, keep * p[k + 1] + weight * (even - odd))
             return carry
 
-        lax.fori_loop(0, width, collide, 0)
-
-        def own_part(x, carry):
-            for c, value in enumerate(sums(lambda k: moved[k, x])):
-                total[c, x + 1] = value
-            return carry
-
-        lax.fori_loop(0, width + 2, own_part, 0)
-
-        def pieces(number):
+        for c in range(CHUNKS):
+            copies[2 + c].wait()
+            for x in range(c * layers, (c + 1) * layers):
+                collide(x, 0)
+
+        def pieces(unit):
+            number, with_pops, with_sums = UNITS[unit]
             sx, sy = DIRECTIONS[number]
             pops, layers, cells = plans[number]
+            pops = pops if with_pops else []
+            layers, cells = (layers, cells) if with_sums else ([], [])
             at, found = 0, []
             from_x = {-1: 0, 0: None, 1: width - 1}[sx]
             from_y = {-1: 0, 0: None, 1: height - 1}[sy]
@@ -225,29 +242,42 @@
                     at += 1
             return found
 
+        remote = {}
+
+        def send(unit):
+            for is_pop, at, length, here, _ in pieces(unit):
+                source = moved if is_pop else total
+                sends[unit][at : at + length, :] = source[here]
+            copy = pltpu.make_async_remote_copy(
+                src_ref=sends[unit],
+                dst_ref=recvs[unit],
+                send_sem=send_sem.at[unit],
+                recv_sem=recv_sem.at[unit],
+                device_id=targets[UNITS[unit][0]],
+                device_id_type=MESH,
+            )
+            copy.start()
+            remote[unit] = copy
+
         pl.semaphore_wait(barrier, 8)
-        remote = []
-        for number in (4, 5, 6, 7, 2, 3, 0, 1):
-            for is_pop, at, length, here, _ in pieces(number):
-                source = moved if is_pop else total
-                sends[number][at : at + length, :] = source[here]
-            copy = pltpu.make_async_remote_copy(
-                src_ref=sends[number],
-                dst_ref=recvs[number],
-                send_sem=send_sem.at[number],
-                recv_sem=recv_sem.at[number],
-                device_id=targets[number],
-                device_id_type=MESH,
-            )
-            copy.start()
-            remote.append((number, copy))
-
-        remote = dict(remote)
-        for number in (0, 1, 4, 5, 6, 7, 2, 3):
-            remote[number].wait_recv()
+        for unit in range(4):
+            send(unit)
+
+        def own_part(x, carry):
+            for c, value in enumerate(sums(lambda k: moved[k, x, 4 : rows - 4, :])):
+                total[c, x + 1, 4 : rows - 4, :] = value
+            return carry
+
+        lax.fori_loop(0, width + 2, own_part, 0, unroll=2)
+
+        for unit in range(4, count):
+            send(unit)
+
+        for unit in (2, 3, 0, 1, 4, 5, 6, 7, 10, 11, 8, 9):
+            remote[unit].wait_recv()
             groups = {}
-            for is_pop, at, length, _, there in pieces(number):
-                value = recvs[number][at : at + length, :]
+            for is_pop, at, length, _, there in pieces(unit):
+                value = recvs[unit][at : at + length, :]
                 if not is_pop:
                     total[there] = total[there] + value
                     continue
@@ -296,12 +326,13 @@
         rows = total.shape[2]
 
         def divide(x, carry):
-            inverse = 1.0 / total[0, x]
+            inverse = 1.0 / total[0, x, 4 : rows - 4, :]
             for a in range(3):
-                flow[a, x, 0:rows, :] = total[a + 1, x] * inverse
-            return carry
-
-        lax.fori_loop(0, width + 5, divide, 0)
+                flow[a, x, 4 : rows - 4, :] = total[a + 1, x, 4 : rows - 4, :] * inverse
+            return carry
+
+        for x in range(width + 5):
+            divide(x, 0)
 
         tall = height + 8
 
@@ -325,7 +356,8 @@
             scaled[x] = (-50.0 / 144.0) * inner
             return carry
 
-        lax.fori_loop(0, width + 1, criterion, 0)
+        for x in range(width + 1):
+            criterion(x, 0)
 
         for copy in copies:
             copy.wait()
@@ -355,7 +387,8 @@
                 cross_out[direction, x] = jnp.where(shown, weight, 0.0)
             return carry
 
-        lax.fori_loop(0, width, edges, 0)
+        for x in range(width):
+            edges(x, 0)
         last = [
             pltpu.make_async_copy(q_out, q_hbm, out_sem.at[1]),
             pltpu.make_async_copy(cross_out, cross_hbm, out_sem.at[2]),
@@ -377,7 +410,7 @@
         rows = PAD + height + 8
         f32 = jnp.float32
         messages = [
-            pltpu.VMEM((message_rows(d, width, height), depth), f32) for d in DIRECTIONS
+            pltpu.VMEM((message_rows(unit, width, height), depth), f32) for unit in UNITS
         ]
         far = pl.BlockSpec(memory_space=pltpu.HBM)
         near = pl.BlockSpec(memory_space=pltpu.VMEM)
@@ -397,9 +430,9 @@
             + messages
             + messages
             + [
-                pltpu.SemaphoreType.DMA((3,)),
-                pltpu.SemaphoreType.DMA((8,)),
-                pltpu.SemaphoreType.DMA((8,)),
+                pltpu.SemaphoreType.DMA((2 + CHUNKS,)),
+                pltpu.SemaphoreType.DMA((len(UNITS),)),
+                pltpu.SemaphoreType.DMA((len(UNITS),)),
             ],
             compiler_params=pltpu.CompilerParams(
                 collective_id=0, has_side_effects=True, vmem_limit_bytes=24 * 1024 * 1024

time: 17.2 us -> 15.7 us (0.913)
  Pallas kernels: 15.6 us -> 14.2 us
    pallas_call x1, Pallas kernels: 13 us -> 12.2 us  [per_device(): pl.pallas_call(kernel_of(sizes, width, height, depth), out_shape=(jax.Sha...]
    pallas_call x1, Pallas kernels: 2.58 us -> 1.93 us  [per_device(): pl.pallas_call(finish_of(width, height, depth), out_shape=(jax.ShapeDtype...]
where the time goes in v3:
time: 15.7 us; the launch traced here: 15.5 us
  Pallas kernels  14.2 us (90%)
  between operations  1.36 us (9%)
    pallas_call x1, Pallas kernels, per_device(): pl.pallas_call(kernel_of(sizes, width, height, depth), out_shape=(jax.Sha...  12.2 us
    pallas_call x1, Pallas kernels, per_device(): pl.pallas_call(finish_of(width, height, depth), out_shape=(jax.ShapeDtype...  1.93 us

profile of v3, /device:TPU:0, one launch (start us, length us, event | category | flops | bytes accessed | tf_op | source)
XLA Modules:
  0.0 15.5 jit_solution(4181832853750591219)
XLA Ops:
  0.6 0.0 copy-start.1
  0.6 0.0 copy-start.2
  0.7 0.0 copy-start
  1.3 12.2 %shard_map.85 = (f32[19,10,32,128]{3,2,1,0:T(8,128)S(1)}, f32[4,13,32,128]{3,2,1,0:T(8,128)S(1)}) custom-call(f32[19,8,16,128]{3,2,1,0:T(8,128)} %pop_hbm.1, s32[8,16,128]{2,1,0:T(8,128)} %solid_hbm.1, f32[1]{0:T(128)S(6)} %copy.9.omega_hbm), custom_call_target="tpu_custom_call" | custom-call | tf_op jit(solution)/shard_map/pallas_call | solution.py:417
  13.6 0.0 copy-done.1
  13.6 0.0 copy-done.2
  13.6 0.0 copy-done
  13.6 1.9 %shard_map.86 = (f32[19,8,16,128]{3,2,1,0:T(8,128)}, f32[8,16,128]{2,1,0:T(8,128)}, f32[3,8,16,128]{3,2,1,0:T(8,128)}) custom-call(f32[19,10,32,128]{3,2,1,0:T(8,128)S(1)} %get-tuple-element.5.moved, f32[4,13,32,128]{3,2,1,0:T(8,128)S(1)} %get-tuple-element.6.total, s32[4,4,8]{2,1,0:T(4,128)S(1)} %copy-done, f32[8]{0:T(128)S(1)} %copy-done.2, ...), custom_call_target="tpu_custom_call" | custom-call | tf_op jit(solution)/shard_map/pallas_call | solution.py:445
Async XLA Ops:
  0.6 12.9 %copy-start.1 = (s32[4,4]{1,0:T(4,128)S(1)}, s32[4,4]{1,0:T(4,128)}, u32[]{:S(2)}) copy-start(s32[4,4]{1,0:T(4,128)} %index_hbm.1) | copy-start | bytes 196
  0.6 12.9 %copy-start.2 = (f32[8]{0:T(128)S(1)}, f32[8]{0:T(128)}, u32[]{:S(2)}) copy-start(f32[8]{0:T(128)} %levels_hbm.1) | copy-start | bytes 100
  0.7 12.9 %copy-start = (s32[4,4,8]{2,1,0:T(4,128)S(1)}, s32[4,4,8]{2,1,0:T(4,128)}, u32[]{:S(2)}) copy-start(s32[4,4,8]{2,1,0:T(4,128)} %visible_hbm.1) | copy-start | bytes 1540

commit v4 on v3

--- a/solution.py
+++ b/solution.py
@@ -72,6 +72,11 @@
     return pops, layers, cells
 
 
+def touches(direction, layer, width, height):
+    sx, sy = direction
+    return layer == (0 if sx + sy < 0 else (width if sx else height) - 1)
+
+
 UNITS = (
     [(number, True, False) for number in (2, 3, 0, 1)]
     + [(number, True, True) for number in (4, 5, 6, 7)]
@@ -86,7 +91,11 @@
     pops = pops if with_pops else []
     layers, cells = (layers, cells) if with_sums else ([], [])
     line = 1 if direction[0] and direction[1] else (height if direction[0] else width)
-    rows = len(pops) * line + 4 * len(layers) * line + 4 * len(cells)
+    rows = len(pops) * line + 4 * len(cells)
+    for layer in layers:
+        rows += 4 * line if touches(direction, layer, width, height) else 3 * line + 2
+    for x, y in cells:
+        rows -= 0 if 0 <= x < width and 0 <= y < height else 1
     return -(-rows // 8) * 8
 
 
@@ -220,10 +229,11 @@
                     here = (k, x, slice(y, y + 1))
                     there = (k, x - sx * width, slice(y - sy * height, y - sy * height + 1))
                     length = 1
-                found.append((True, at, length, here, there))
+                found.append(("pop", at, length, here, there))
                 at += length
             for layer in layers:
-                for c in range(4):
+                whole = touches(DIRECTIONS[number], layer, width, height)
+                for c in range(0 if whole else 1, 4):
                     if sy == 0:
                         y = slice(PAD, PAD + height)
                         here, there = (c, layer + 2, y), (c, layer + 2 - sx * width, y)
@@ -232,22 +242,48 @@
                         here = (c, slice(2, 2 + width), PAD + layer)
                         there = (c, slice(2, 2 + width), PAD + layer - sy * height)
                         length = width
-                    found.append((False, at, length, here, there))
+                    found.append(("sum" if whole else "flow", at, length, here, there))
                     at += length
+                for edge in () if whole else (0, (height if sy == 0 else width) - 1):
+                    x, y = (layer, edge) if sy == 0 else (edge, layer)
+                    row = slice(PAD + y, PAD + y + 1)
+                    to = PAD + y - sy * height
+                    there = (0, x + 2 - sx * width, slice(to, to + 1))
+                    found.append(("sum", at, 1, (0, x + 2, row), there))
+                    at += 1
             for x, y in cells:
                 for c in range(4):
+                    if (c == 1 and not 0 <= x < width) or (c == 2 and not 0 <= y < height):
+                        continue
                     here = (c, x + 2, slice(PAD + y, PAD + y + 1))
                     to = PAD + y - sy * height
-                    found.append((False, at, 1, here, (c, x + 2 - sx * width, slice(to, to + 1))))
+                    there = (c, x + 2 - sx * width, slice(to, to + 1))
+                    kind = "sum"
+                    if c == 0 and not 0 <= x < width:
+                        kind = ("also", 1, x < 0)
+                    if c == 0 and not 0 <= y < height:
+                        kind = ("also", 2, y < 0)
+                    found.append((kind, at, 1, here, there))
                     at += 1
             return found
 
         remote = {}
 
+        def inner(length):
+            place = lax.broadcasted_iota(jnp.int32, (length, depth), 0)
+            return jnp.logical_and(place > 0, place < length - 1)
+
         def send(unit):
-            for is_pop, at, length, here, _ in pieces(unit):
-                source = moved if is_pop else total
-                sends[unit][at : at + length, :] = source[here]
+            inverses = {}
+            for kind, at, length, here, _ in pieces(unit):
+                value = moved[here] if kind == "pop" else total[here]
+                if kind == "flow":
+                    key = str(here[1:])
+                    if key not in inverses:
+                        density = total[(0,) + here[1:]]
+                        inverses[key] = jnp.where(inner(length), 1.0 / density, 1.0)
+                    value = value * inverses[key]
+                sends[unit][at : at + length, :] = value
             copy = pltpu.make_async_remote_copy(
                 src_ref=sends[unit],
                 dst_ref=recvs[unit],
@@ -276,10 +312,16 @@
         for unit in (2, 3, 0, 1, 4, 5, 6, 7, 10, 11, 8, 9):
             remote[unit].wait_recv()
             groups = {}
-            for is_pop, at, length, _, there in pieces(unit):
+            for kind, at, length, _, there in pieces(unit):
                 value = recvs[unit][at : at + length, :]
-                if not is_pop:
+                if kind != "pop":
                     total[there] = total[there] + value
+                    if kind == "flow" and there[0] == 1:
+                        density = (0,) + there[1:]
+                        total[density] = total[density] + jnp.where(inner(length), 1.0, 0.0)
+                    if kind[0] == "also":
+                        c = (kind[1],) + there[1:]
+                        total[c] = total[c] + (-value if kind[2] else value)
                     continue
                 moved[there] = value
                 k, x, y = there

time: 15.7 us -> 15.1 us (0.962)
  Pallas kernels: 14.2 us -> 13.6 us
    pallas_call x1, Pallas kernels: 12.2 us -> 11.6 us  [per_device(): pl.pallas_call(kernel_of(sizes, width, height, depth), out_shape=(jax.Sha...]
where the time goes in v4:
time: 15.1 us; the launch traced here: 14.9 us
  Pallas kernels  13.6 us (90%)
  between operations  1.36 us (9%)
    pallas_call x1, Pallas kernels, per_device(): pl.pallas_call(kernel_of(sizes, width, height, depth), out_shape=(jax.Sha...  11.6 us
    pallas_call x1, Pallas kernels, per_device(): pl.pallas_call(finish_of(width, height, depth), out_shape=(jax.ShapeDtype...  1.93 us

profile of v4, /device:TPU:0, one launch (start us, length us, event | category | flops | bytes accessed | tf_op | source)
XLA Modules:
  0.0 14.9 jit_solution(11831262081553968351)
XLA Ops:
  0.6 0.0 copy-start.1
  0.6 0.0 copy-start.2
  0.7 0.0 copy-start
  1.3 11.6 %shard_map.85 = (f32[19,10,32,128]{3,2,1,0:T(8,128)S(1)}, f32[4,13,32,128]{3,2,1,0:T(8,128)S(1)}) custom-call(f32[19,8,16,128]{3,2,1,0:T(8,128)} %pop_hbm.1, s32[8,16,128]{2,1,0:T(8,128)} %solid_hbm.1, f32[1]{0:T(128)S(6)} %copy.9.omega_hbm), custom_call_target="tpu_custom_call" | custom-call | tf_op jit(solution)/shard_map/pallas_call | solution.py:459
  13.0 0.0 copy-done.1
  13.0 0.0 copy-done.2
  13.0 0.0 copy-done
  13.0 1.9 %shard_map.86 = (f32[19,8,16,128]{3,2,1,0:T(8,128)}, f32[8,16,128]{2,1,0:T(8,128)}, f32[3,8,16,128]{3,2,1,0:T(8,128)}) custom-call(f32[19,10,32,128]{3,2,1,0:T(8,128)S(1)} %get-tuple-element.5.moved, f32[4,13,32,128]{3,2,1,0:T(8,128)S(1)} %get-tuple-element.6.total, s32[4,4,8]{2,1,0:T(4,128)S(1)} %copy-done, f32[8]{0:T(128)S(1)} %copy-done.2, ...), custom_call_target="tpu_custom_call" | custom-call | tf_op jit(solution)/shard_map/pallas_call | solution.py:487
Async XLA Ops:
  0.6 12.3 %copy-start.1 = (s32[4,4]{1,0:T(4,128)S(1)}, s32[4,4]{1,0:T(4,128)}, u32[]{:S(2)}) copy-start(s32[4,4]{1,0:T(4,128)} %index_hbm.1) | copy-start | bytes 196
  0.6 12.3 %copy-start.2 = (f32[8]{0:T(128)S(1)}, f32[8]{0:T(128)}, u32[]{:S(2)}) copy-start(f32[8]{0:T(128)} %levels_hbm.1) | copy-start | bytes 100
  0.7 12.3 %copy-start = (s32[4,4,8]{2,1,0:T(4,128)S(1)}, s32[4,4,8]{2,1,0:T(4,128)}, u32[]{:S(2)}) copy-start(s32[4,4,8]{2,1,0:T(4,128)} %visible_hbm.1) | copy-start | bytes 1540

commit v5 on v4

--- a/solution.py
+++ b/solution.py
@@ -118,7 +118,7 @@
     size_x, size_y = sizes
     plans = [message_plan(d, width, height) for d in DIRECTIONS]
 
-    def kernel(pop_hbm, solid_hbm, omega_hbm, moved, total, pop, solid, omega, *rest):
+    def kernel(pop_hbm, solid_hbm, omega_rows, moved, total, pop, solid, *rest):
         count = len(UNITS)
         sends, recvs = rest[:count], rest[count : 2 * count]
         in_sem, send_sem, recv_sem = rest[2 * count :]
@@ -127,15 +127,13 @@
         copies = [
             pltpu.make_async_copy(src, dst, in_sem.at[i])
             for i, (src, dst) in enumerate(
-                [(solid_hbm, solid), (omega_hbm, omega)]
+                [(solid_hbm, solid)]
                 + [
                     (pop_hbm.at[:, pl.ds(c * layers, layers)], pop.at[:, pl.ds(c * layers, layers)])
                     for c in range(CHUNKS)
                 ]
             )
         ]
-        for copy in copies:
-            copy.start()
         targets = [
             (lax.rem(ix + sx + size_x, size_x), lax.rem(iy + sy + size_y, size_y))
             for sx, sy in DIRECTIONS
@@ -143,6 +141,8 @@
         barrier = pltpu.get_barrier_semaphore()
         for target in targets:
             pl.semaphore_signal(barrier, inc=1, device_id=target, device_id_type=MESH)
+        for copy in copies:
+            copy.start()
 
         rows = moved.shape[2]
         blank = jnp.zeros((rows, depth), jnp.float32)
@@ -156,10 +156,10 @@
         for x in (0, width + 3, width + 4):
             for c in range(4):
                 total[c, x] = blank
-        for copy in copies[:2]:
+        for copy in copies[:1]:
             copy.wait()
 
-        rate = omega[0]
+        rate = omega_rows[0:1, :]
         keep = 1.0 - rate
 
         def collide(x, carry):
@@ -200,7 +200,7 @@
             return carry
 
         for c in range(CHUNKS):
-            copies[2 + c].wait()
+            copies[1 + c].wait()
             for x in range(c * layers, (c + 1) * layers):
                 collide(x, 0)
 
@@ -462,17 +462,16 @@
                 jax.ShapeDtypeStruct((19, width + 2, rows, depth), f32),
                 jax.ShapeDtypeStruct((4, width + 5, rows, depth), f32),
             ),
-            in_specs=[far] * 3,
+            in_specs=[far, far, near],
             out_specs=(near, near),
             scratch_shapes=[
                 pltpu.VMEM(populations.shape, f32),
                 pltpu.VMEM(solid.shape, jnp.int32),
-                pltpu.SMEM(omega.shape, f32),
             ]
             + messages
             + messages
             + [
-                pltpu.SemaphoreType.DMA((2 + CHUNKS,)),
+                pltpu.SemaphoreType.DMA((1 + CHUNKS,)),
                 pltpu.SemaphoreType.DMA((len(UNITS),)),
                 pltpu.SemaphoreType.DMA((len(UNITS),)),
             ],
@@ -482,7 +481,7 @@
         )(
             pltpu.with_memory_space_constraint(populations, pltpu.HBM),
             pltpu.with_memory_space_constraint(solid, pltpu.HBM),
-            omega,
+            jnp.broadcast_to(omega, (8, depth)),
         )
         return pl.pallas_call(
             finish_of(width, height, depth),

time: 15.1 us -> 15.1 us (level)
  no operation moved by 1% of the time
where the time goes in v5:
time: 15.1 us; the launch traced here: 14.9 us
  Pallas kernels  13.6 us (90%)
  between operations  1.36 us (9%)
    pallas_call x1, Pallas kernels, per_device(): pl.pallas_call(kernel_of(sizes, width, height, depth), out_shape=(jax.Sha...  11.6 us
    pallas_call x1, Pallas kernels, per_device(): pl.pallas_call(finish_of(width, height, depth), out_shape=(jax.ShapeDtype...  1.94 us

profile of v5, /device:TPU:0, one launch (start us, length us, event | category | flops | bytes accessed | tf_op | source)
XLA Modules:
  0.0 14.9 jit_solution(8150910941005484938)
XLA Ops:
  0.6 0.0 copy-start.1
  0.6 0.0 copy-start.2
  0.7 0.0 copy-start
  1.3 11.6 %shard_map.88 = (f32[19,10,32,128]{3,2,1,0:T(8,128)S(1)}, f32[4,13,32,128]{3,2,1,0:T(8,128)S(1)}) custom-call(f32[19,8,16,128]{3,2,1,0:T(8,128)} %pop_hbm.1, s32[8,16,128]{2,1,0:T(8,128)} %solid_hbm.1, f32[8,128]{1,0:T(8,128)S(1)} %broadcast_in_dim.2.omega_rows), custom_call_target="tpu_custom_call" | custom-call | tf_op jit(solution)/shard_map/pallas_call | solution.py:459
  13.0 0.0 copy-done.1
  13.0 0.0 copy-done.2
  13.0 0.0 copy-done
  13.0 1.9 %shard_map.89 = (f32[19,8,16,128]{3,2,1,0:T(8,128)}, f32[8,16,128]{2,1,0:T(8,128)}, f32[3,8,16,128]{3,2,1,0:T(8,128)}) custom-call(f32[19,10,32,128]{3,2,1,0:T(8,128)S(1)} %get-tuple-element.5.moved, f32[4,13,32,128]{3,2,1,0:T(8,128)S(1)} %get-tuple-element.6.total, s32[4,4,8]{2,1,0:T(4,128)S(1)} %copy-done, f32[8]{0:T(128)S(1)} %copy-done.2, ...), custom_call_target="tpu_custom_call" | custom-call | tf_op jit(solution)/shard_map/pallas_call | solution.py:486
  (1 shorter events, 0.0 us)
Async XLA Ops:
  0.6 12.4 %copy-start.1 = (s32[4,4]{1,0:T(4,128)S(1)}, s32[4,4]{1,0:T(4,128)}, u32[]{:S(2)}) copy-start(s32[4,4]{1,0:T(4,128)} %index_hbm.1) | copy-start | bytes 196
  0.6 12.4 %copy-start.2 = (f32[8]{0:T(128)S(1)}, f32[8]{0:T(128)}, u32[]{:S(2)}) copy-start(f32[8]{0:T(128)} %levels_hbm.1) | copy-start | bytes 100
  0.7 12.4 %copy-start = (s32[4,4,8]{2,1,0:T(4,128)S(1)}, s32[4,4,8]{2,1,0:T(4,128)}, u32[]{:S(2)}) copy-start(s32[4,4,8]{2,1,0:T(4,128)} %visible_hbm.1) | copy-start | bytes 1540

commit v6 on v5

--- a/solution.py
+++ b/solution.py
@@ -79,8 +79,9 @@
 
 UNITS = (
     [(number, True, False) for number in (2, 3, 0, 1)]
+    + [(number, False, True) for number in (2, 3)]
     + [(number, True, True) for number in (4, 5, 6, 7)]
-    + [(number, False, True) for number in (2, 3, 0, 1)]
+    + [(number, False, True) for number in (0, 1)]
 )
 
 
@@ -304,12 +305,13 @@
                 total[c, x + 1, 4 : rows - 4, :] = value
             return carry
 
-        lax.fori_loop(0, width + 2, own_part, 0, unroll=2)
+        for x in range(width + 2):
+            own_part(x, 0)
 
         for unit in range(4, count):
             send(unit)
 
-        for unit in (2, 3, 0, 1, 4, 5, 6, 7, 10, 11, 8, 9):
+        for unit in (2, 3, 0, 1, 6, 7, 8, 9, 10, 11, 4, 5):
             remote[unit].wait_recv()
             groups = {}
             for kind, at, length, _, there in pieces(unit):

time: 15.1 us -> 16.3 us (1.079)
  Pallas kernels: 13.6 us -> 14.7 us
    pallas_call x1, Pallas kernels: 11.6 us -> 12.8 us  [per_device(): pl.pallas_call(kernel_of(sizes, width, height, depth), out_shape=(jax.Sha...]
where the time goes in v6:
time: 16.3 us; the launch traced here: 16.1 us
  Pallas kernels  14.7 us (90%)
  between operations  1.36 us (8%)
    pallas_call x1, Pallas kernels, per_device(): pl.pallas_call(kernel_of(sizes, width, height, depth), out_shape=(jax.Sha...  12.8 us
    pallas_call x1, Pallas kernels, per_device(): pl.pallas_call(finish_of(width, height, depth), out_shape=(jax.ShapeDtype...  1.94 us

profile of v6, /device:TPU:0, one launch (start us, length us, event | category | flops | bytes accessed | tf_op | source)
XLA Modules:
  0.0 16.1 jit_solution(106280519253492441)
XLA Ops:
  0.6 0.0 copy-start.1
  0.6 0.0 copy-start.2
  0.7 0.0 copy-start
  1.3 12.8 %shard_map.88 = (f32[19,10,32,128]{3,2,1,0:T(8,128)S(1)}, f32[4,13,32,128]{3,2,1,0:T(8,128)S(1)}) custom-call(f32[19,8,16,128]{3,2,1,0:T(8,128)} %pop_hbm.1, s32[8,16,128]{2,1,0:T(8,128)} %solid_hbm.1, f32[8,128]{1,0:T(8,128)S(1)} %broadcast_in_dim.2.omega_rows), custom_call_target="tpu_custom_call" | custom-call | tf_op jit(solution)/shard_map/pallas_call | solution.py:461
  14.2 0.0 copy-done.1
  14.2 0.0 copy-done.2
  14.2 0.0 copy-done
  14.2 1.9 %shard_map.89 = (f32[19,8,16,128]{3,2,1,0:T(8,128)}, f32[8,16,128]{2,1,0:T(8,128)}, f32[3,8,16,128]{3,2,1,0:T(8,128)}) custom-call(f32[19,10,32,128]{3,2,1,0:T(8,128)S(1)} %get-tuple-element.5.moved, f32[4,13,32,128]{3,2,1,0:T(8,128)S(1)} %get-tuple-element.6.total, s32[4,4,8]{2,1,0:T(4,128)S(1)} %copy-done, f32[8]{0:T(128)S(1)} %copy-done.2, ...), custom_call_target="tpu_custom_call" | custom-call | tf_op jit(solution)/shard_map/pallas_call | solution.py:488
  (1 shorter events, 0.0 us)
Async XLA Ops:
  0.6 13.5 %copy-start.1 = (s32[4,4]{1,0:T(4,128)S(1)}, s32[4,4]{1,0:T(4,128)}, u32[]{:S(2)}) copy-start(s32[4,4]{1,0:T(4,128)} %index_hbm.1) | copy-start | bytes 196
  0.6 13.5 %copy-start.2 = (f32[8]{0:T(128)S(1)}, f32[8]{0:T(128)}, u32[]{:S(2)}) copy-start(f32[8]{0:T(128)} %levels_hbm.1) | copy-start | bytes 100
  0.7 13.5 %copy-start = (s32[4,4,8]{2,1,0:T(4,128)S(1)}, s32[4,4,8]{2,1,0:T(4,128)}, u32[]{:S(2)}) copy-start(s32[4,4,8]{2,1,0:T(4,128)} %visible_hbm.1) | copy-start | bytes 1540
